TPU v7x, 32 devices: a whole 2x2x4 slice. The times are simulated.
32 devices in a mesh: grp: 4 (over z), blk: 8 (over y, x, core).
Axes of the slice: x: 2, y: 2, z: 4, core: 2. Of those that a mesh axis runs over, the one named last changes fastest.
Arguments:
- slab: bfloat16 [16, 2048, 2048], P('grp', 'blk'), may hold values from -0.59765625 to 0.59765625
- block_mask: int32 [4, 64, 64], P('grp', 'blk'), may hold values 0 or 1
- orbitals: bfloat16 [2048, 1024], P('blk'), may hold values from -0.125 to 0.125
- margin: bfloat16 [2048, 2048], P('blk', 'grp'), as said below
- env_flag: int32 [1024], replicated, may hold values from 0 to 1
Outputs:
- projected: float32 [2048, 2048], P('blk', 'grp')
Inputs may be any that keep to these rules, and one draw needn't show every extreme that they name: margin is symmetric positive definite with unit diagonal.
All inputs are finite; a program needn't handle non-finite values. No bound on the sum of `block_mask` on one device may be relied on, other than what follows from the above.
Results may differ from a plain program's by a relative error of at most 0.003.
Values may be sent and summed in bfloat16 or wider, within the bound.
A program may use at most 128 MiB of HBM per device.

v0:
```python
import jax
import jax.numpy as jnp
from jax import lax
from jax.sharding import PartitionSpec as P

ATILE = 32


def inner_rows(left, right):
    return lax.dot_general(
        left, right, (((0,), (0,)), ((), ())), preferred_element_type=jnp.float32
    )


def pair_block(half, other):
    return jnp.einsum("pmi,pni->mn", half, other, preferred_element_type=jnp.float32)


def on_device(slab, block_mask, orbitals, margin, env_flag):
    aux_dev, ao_dev, nao = slab.shape
    keep_tile = jnp.repeat(jnp.repeat(block_mask[0], ATILE, axis=0), ATILE, axis=1).astype(
        jnp.bfloat16
    )
    masked = slab * keep_tile[None, :, :]
    whole_c = lax.all_gather(orbitals, "blk", axis=0, tiled=True)
    occ = whole_c.shape[1]
    half = jnp.dot(
        masked.reshape(aux_dev * ao_dev, nao), whole_c, preferred_element_type=jnp.float32
    )
    half = half.astype(jnp.bfloat16).reshape(aux_dev, ao_dev, occ)
    position = lax.axis_index("blk")
    rows_k = pair_block(half, lax.all_gather(half, "blk", axis=1, tiled=True))
    k_tile = lax.psum_scatter(rows_k, "grp", scatter_dimension=1, tiled=True)
    width = k_tile.shape[1]
    ce_whole = whole_c * env_flag.astype(jnp.bfloat16)[None, :]
    ce_rows = lax.dynamic_slice_in_dim(ce_whole, position * ao_dev, ao_dev, 0)
    ce_cols = lax.dynamic_slice_in_dim(ce_whole, lax.axis_index("grp") * width, width, 0)
    k_bf = k_tile.astype(jnp.bfloat16)
    left_part = inner_rows(ce_rows, k_bf)
    envov_part = inner_rows(ce_rows, margin)
    left_env, env_margin = lax.psum((left_part, envov_part), "blk")
    right_part = jnp.dot(k_bf, ce_cols, preferred_element_type=jnp.float32)
    ovenv_part = jnp.dot(margin, ce_cols, preferred_element_type=jnp.float32)
    right_env, margin_env = lax.psum((right_part, ovenv_part), "grp")
    first = jnp.dot(
        margin_env.astype(jnp.bfloat16),
        left_env.astype(jnp.bfloat16),
        preferred_element_type=jnp.float32,
    )
    second = jnp.dot(
        right_env.astype(jnp.bfloat16),
        env_margin.astype(jnp.bfloat16),
        preferred_element_type=jnp.float32,
    )
    return k_tile - first - second


def solution(mesh):
    placed = (P("grp", "blk", None), P("grp", "blk", None), P("blk", None), P("blk", "grp"), P())
    return jax.shard_map(
        on_device, mesh=mesh, in_specs=placed, out_specs=P("blk", "grp"), check_vma=False
    )
```

profile of v0, /device:TPU:0, one launch (start us, length us, event | category | flops | bytes accessed | tf_op | source)
XLA Modules:
  0.0 383.1 jit_solution(16578461635682286219)
XLA Ops:
  6.5 0.0 copy-start
  6.5 0.0 all-gather.3.cloned.1.call-start
  6.5 0.7 all-gather.3.cloned.1.call-update
  7.3 0.0 all-gather.5.cloned.1.call-start
  7.3 0.7 convert_bitcast_fusion
  8.0 0.1 copy.8
  8.1 0.1 broadcast_in_dim.9
  8.2 0.6 copy.9
  8.8 4.6 %broadcast_multiply_fusion.1 = bf16[4,256,2048]{2,1,0:T(8,128)(2,1)} fusion(bf16[4,256,2048]{2,1,0:T(8,128)(2,1)} %param.5, bf16[256,2048]{1,0:T(8,128)(2,1)S(1)} %copy.9), kind=kLoop, calls=%fused_computation.2 | loop fusion | flops 2097152 | bytes 9437184 | tf_op jit(solution)/shard_map/mul | solution.py:24
  13.4 35.3 %all-gather.3.cloned.1.call-done = bf16[2048,1024]{1,0:T(8,128)(2,1)} async-done(((bf16[256,1024]{1,0:T(8,128)(2,1)}), bf16[2048,1024]{1,0:T(8,128)(2,1)}) %all-gather.3.cloned.1.call-update) | async-done | bytes 4194320 | tf_op jit(solution)/shard_map/all_gather | solution.py:25
  48.7 9.3 %convolution_convert_fusion = bf16[1024,1024]{1,0:T(8,128)(2,1)} fusion(bf16[1024,2048]{1,0:T(8,128)(2,1)} %bitcast.20, bf16[2048,1024]{1,0:T(8,128)(2,1)} %all-gather.3.cloned.1.call-done), kind=kOutput, calls=%fused_computation.3 | convolution fusion | flops 4296015872 | bytes 10485760 | tf_op jit(solution)/shard_map/dot_general | solution.py:27
  58.0 0.0 all-gather.5.cloned.1.call-update
  58.0 0.0 copy-start.4
  58.0 0.0 reduce-scatter.2.cloned.1.call-start
  58.1 90.0 %all-gather.5.cloned.1.call-done = bf16[4,2048,1024]{2,1,0:T(8,128)(2,1)} async-done(((bf16[4,256,1024]{2,1,0:T(8,128)(2,1)}), bf16[4,2048,1024]{2,1,0:T(8,128)(2,1)}) %all-gather.5.cloned.1.call-update) | async-done | bytes 16777232 | tf_op jit(solution)/shard_map/all_gather | solution.py:32
  148.0 12.3 %convolution_bitcast_fusion = f32[256,2048]{1,0:T(8,128)} fusion(bf16[4,256,1024]{2,1,0:T(8,128)(2,1)} %bitcast.23, bf16[4,2048,1024]{2,1,0:T(8,128)(2,1)} %all-gather.5.cloned.1.call-done), kind=kOutput, calls=%fused_computation | convolution fusion | flops 4294967296 | bytes 20971520 | tf_op jit(solution)/shard_map/pmi,pni->mn/dot_general | solution.py:16
  160.3 0.0 reduce-scatter.2.cloned.1.call-update
  160.3 0.0 copy-done.4
  160.4 2.5 broadcast_multiply_fusion
  162.8 0.0 copy-done
  162.8 0.0 copy-start.1
  162.8 0.5 fusion.7
  163.3 1.5 copy-done.1
  164.8 1.5 convolution_bitcast_fusion.1
  166.3 38.1 %reduce-scatter.2.cloned.1.call-done = f32[256,512]{1,0:T(8,128)} async-done(((f32[256,2048]{1,0:T(8,128)}), f32[256,512]{1,0:T(8,128)}) %reduce-scatter.2.cloned.1.call-update) | async-done | bytes 524304 | tf_op jit(solution)/shard_map/reduce_scatter | solution.py:33
  204.3 3.0 fusion.9
  207.3 0.0 copy-start.2
  207.3 2.9 fusion.2
  210.2 88.3 %all-reduce.4 = (bf16[1024,512]{1,0:T(8,128)(2,1)}, bf16[1024,512]{1,0:T(8,128)(2,1)}) all-reduce(f32[1024,512]{1,0:T(8,128)} %fusion.9, f32[1024,512]{1,0:T(8,128)S(1)} %fusion.7), channel_id=1, replica_groups=mesh['grp'=4,'blk'=8] {'blk'}, use_global_device_ids=true, to_apply=%region_2.0 | all-reduce | flops 1048576 | bytes 6291456 | tf_op jit(solution)/shard_map/psum | solution.py:41
  298.5 0.0 copy-start.3
  298.5 75.1 %all-reduce.5 = (bf16[256,1024]{0,1:T(8,128)(2,1)S(1)}, bf16[256,1024]{1,0:T(8,128)(2,1)S(1)}) all-reduce(f32[256,1024]{0,1:T(8,128)} %convolution_bitcast_fusion.1, f32[256,1024]{1,0:T(8,128)} %fusion.2), channel_id=1, replica_groups=mesh['grp'=4,'blk'=8] {'grp'}, use_global_device_ids=true, to_apply=%region_1.0 | all-reduce | flops 524288 | bytes 3145728 | tf_op jit(solution)/shard_map/psum | solution.py:44
  373.6 0.0 copy-done.2
  373.6 1.7 convolution_subtract_fusion.1
  375.3 0.0 copy-done.3
  375.3 1.2 convolution_subtract_fusion
  (2 shorter events, 0.0 us)
Async XLA Ops:
  6.5 156.3 %copy-start = (bf16[256,512]{1,0:T(8,128)(2,1)S(1)}, bf16[256,512]{1,0:T(8,128)(2,1)}, u32[]{:S(2)}) copy-start(bf16[256,512]{1,0:T(8,128)(2,1)} %param.8) | copy-start | bytes 786436
  6.5 42.2 %all-gather.3.cloned.1.call-start = ((), (), s32[]{:S(2)}) async-start(), calls=%async_computation.1 | async-start | bytes 4718592 | tf_op jit(solution)/shard_map/all_gather | solution.py:25
  7.3 140.8 %all-gather.5.cloned.1.call-start = ((), (), s32[]{:S(2)}) async-start(), calls=%async_computation.2 | async-start | bytes 18874368 | tf_op jit(solution)/shard_map/all_gather | solution.py:32
  58.0 102.3 %copy-start.4 = (s32[1024]{0:T(1024)S(1)}, s32[1024]{0:T(1024)}, u32[]{:S(2)}) copy-start(s32[1024]{0:T(1024)} %param.9) | copy-start | bytes 12292
  58.0 146.3 %reduce-scatter.2.cloned.1.call-start = ((), (), s32[]{:S(2)}) async-start(), calls=%async_computation.3 | async-start | bytes 2621440 | tf_op jit(solution)/shard_map/reduce_scatter | solution.py:33
  162.8 1.9 copy-start.1
  207.3 166.3 %copy-start.2 = (f32[256,512]{1,0:T(8,128)S(1)}, f32[256,512]{1,0:T(8,128)}, u32[]{:S(2)}) copy-start(f32[256,512]{1,0:T(8,128)} %reduce-scatter.2.cloned.1.call-done) | copy-start | bytes 1572868
  298.5 76.8 %copy-start.3 = (bf16[1024,512]{1,0:T(8,128)(2,1)S(1)}, bf16[1024,512]{1,0:T(8,128)(2,1)}, u32[]{:S(2)}) copy-start(bf16[1024,512]{1,0:T(8,128)(2,1)} %get-tuple-element.6) | copy-start | bytes 3145732
Sparse Core Ops, SparseCore 0:
  9.2 39.4 all-gather.2
  58.2 89.8 all-gather.4
  160.4 43.8 reduce-scatter.1
where the time goes:
time: 383 us
  waiting for transfers between devices  164 us (43%)
  blocking collectives  163 us (43%)
  matrix products  32.3 us (8%)
  between operations  13.2 us (3%)
  other arithmetic  7.71 us (2%)
    all_gather x1, waiting for transfers between devices, on_device(): rows_k = pair_block(half, lax.all_gather(half, 'blk', axis=1, tiled=True))  90 us
    psum x1, blocking collectives, on_device(): left_env, env_margin = lax.psum((left_part, envov_part), 'blk')  88.3 us
    psum x1, blocking collectives, on_device(): right_env, margin_env = lax.psum((right_part, ovenv_part), 'grp')  75.1 us
    reduce_scatter x1, waiting for transfers between devices, on_device(): k_tile = lax.psum_scatter(rows_k, 'grp', scatter_dimension=1, tiled=True)  38.1 us
    all_gather x1, waiting for transfers between devices, on_device(): whole_c = lax.all_gather(orbitals, 'blk', axis=0, tiled=True)  35.3 us
    dot_general x1, matrix products, pair_block(): jnp.einsum('pmi,pni->mn', half, other, preferred_element_type=jnp.float32)  12.3 us
    dot_general x1, matrix products, on_device(): jnp.dot(masked.reshape(aux_dev * ao_dev, nao), whole_c, preferred_element...  9.31 us
  transfers between devices with their start and end apart: 3, of which 3 were waited for; matrix products, arithmetic and copies ran while one was open for 3% of the time, Pallas kernels for 0%

commit v1 on v0

v1 whole, which is shorter than its diff:
```python
import jax
import jax.numpy as jnp
from jax import lax
from jax.sharding import PartitionSpec as P

ATILE = 32


def dot32(left, right, dims):
    return lax.dot_general(left, right, (dims, ((), ())), preferred_element_type=jnp.float32)


def pair_block(half, other):
    return jnp.einsum("pmi,pni->mn", half, other, preferred_element_type=jnp.float32)


def on_device(slab, block_mask, orbitals, margin, env_flag):
    bf16 = jnp.bfloat16
    aux_dev, ao_dev, nao = slab.shape
    keep_tile = jnp.repeat(jnp.repeat(block_mask[0], ATILE, axis=0), ATILE, axis=1).astype(bf16)
    masked = slab * keep_tile[None, :, :]
    whole_c = lax.all_gather(orbitals, "blk", axis=0, tiled=True)
    margin_rows = lax.all_gather(margin, "grp", axis=1, tiled=True)
    margin_cols = lax.all_gather(margin, "blk", axis=0, tiled=True)
    occ = whole_c.shape[1]
    half = jnp.dot(
        masked.reshape(aux_dev * ao_dev, nao), whole_c, preferred_element_type=jnp.float32
    )
    half = half.astype(bf16).reshape(aux_dev, ao_dev, occ)
    rows_k = pair_block(half, lax.all_gather(half, "blk", axis=1, tiled=True))
    env = whole_c * env_flag.astype(bf16)[None, :]
    t_rows = dot32(dot32(margin_rows, env, ((1,), (0,))).astype(bf16), env, ((1,), (1,))).astype(bf16)
    t_cols = dot32(dot32(margin_cols, env, ((0,), (0,))).astype(bf16), env, ((1,), (1,))).astype(bf16)
    k_tile = lax.psum_scatter(rows_k, "grp", scatter_dimension=1, tiled=True)
    k_bf = k_tile.astype(bf16)
    k_cols = lax.all_gather(k_bf, "blk", axis=0, tiled=True)
    k_rows = lax.all_gather(k_bf, "grp", axis=1, tiled=True)
    first = dot32(t_rows, k_cols, ((1,), (0,)))
    second = dot32(k_rows, t_cols, ((1,), (1,)))
    return k_tile - first - second


def solution(mesh):
    placed = (P("grp", "blk", None), P("grp", "blk", None), P("blk", None), P("blk", "grp"), P())
    return jax.shard_map(
        on_device, mesh=mesh, in_specs=placed, out_specs=P("blk", "grp"), check_vma=False
    )
```

time: 383 us -> 332 us (0.87)
  blocking collectives: 163 us -> 0 us
  waiting for transfers between devices: 164 us -> 265 us
  matrix products: 32.3 us -> 44.8 us
    psum x2 -> x0, blocking collectives: 163 us -> none  [the longest x1 88.3 us: on_device(): left_env, env_margin = lax.psum((left_part, envov_part), 'blk')]
    all_gather x0 -> x4, waiting for transfers between devices: none -> 94.5 us  [the longest x1 27 us: on_device(): k_rows = lax.all_gather(k_bf, 'grp', axis=1, tiled=True)]
    dot_general x6 -> x4, matrix products: 10.7 us -> 23.2 us  [dot32(): lax.dot_general(left, right, (dims, ((), ())), preferred_element_type=jnp...]
    reduce_scatter x1, waiting for transfers between devices: 38.1 us -> 42.8 us  [on_device(): k_tile = lax.psum_scatter(rows_k, 'grp', scatter_dimension=1, tiled=True)]
  transfers between devices with their start and end apart: 3 -> 7, of which waited for: 3 -> 7; matrix products, arithmetic and copies ran while one was open for 3% -> 9% of each run, Pallas kernels for 0% -> 0%
where the time goes in v1:
time: 332 us
  waiting for transfers between devices  265 us (80%)
  matrix products  44.8 us (13%)
  between operations  13.6 us (4%)
  other arithmetic  7.03 us (2%)
    all_gather x1, waiting for transfers between devices, on_device(): rows_k = pair_block(half, lax.all_gather(half, 'blk', axis=1, tiled=True))  90 us
    reduce_scatter x1, waiting for transfers between devices, on_device(): k_tile = lax.psum_scatter(rows_k, 'grp', scatter_dimension=1, tiled=True)  42.8 us
    all_gather x1, waiting for transfers between devices, on_device(): whole_c = lax.all_gather(orbitals, 'blk', axis=0, tiled=True)  35.3 us
    all_gather x1, waiting for transfers between devices, on_device(): k_rows = lax.all_gather(k_bf, 'grp', axis=1, tiled=True)  27 us
    all_gather x1, waiting for transfers between devices, on_device(): margin_rows = lax.all_gather(margin, 'grp', axis=1, tiled=True)  26.3 us
    dot_general x4, matrix products, dot32(): lax.dot_general(left, right, (dims, ((), ())), preferred_element_type=jnp...  23.2 us
    all_gather x1, waiting for transfers between devices, on_device(): k_cols = lax.all_gather(k_bf, 'blk', axis=0, tiled=True)  21.2 us
    all_gather x1, waiting for transfers between devices, on_device(): margin_cols = lax.all_gather(margin, 'blk', axis=0, tiled=True)  20.1 us
  transfers between devices with their start and end apart: 7, of which 7 were waited for; matrix products, arithmetic and copies ran while one was open for 9% of the time, Pallas kernels for 0%

profile of v1, /device:TPU:0, one launch (start us, length us, event | category | flops | bytes accessed | tf_op | source)
XLA Modules:
  0.0 331.5 jit_solution(11862065166852818804)
XLA Ops:
  6.5 0.0 all-gather.7.cloned.1.call-start
  6.5 0.7 all-gather.7.cloned.1.call-update
  7.3 0.0 all-gather.9.cloned.1.call-start
  7.3 0.7 convert_bitcast_fusion
  8.0 0.1 copy.8
  8.1 0.1 broadcast_in_dim.9
  8.2 0.6 copy.9
  8.8 4.6 %broadcast_multiply_fusion = bf16[4,256,2048]{2,1,0:T(8,128)(2,1)} fusion(bf16[4,256,2048]{2,1,0:T(8,128)(2,1)} %param.5, bf16[256,2048]{1,0:T(8,128)(2,1)S(1)} %copy.9), kind=kLoop, calls=%fused_computation.14 | loop fusion | flops 2097152 | bytes 9437184 | tf_op jit(solution)/shard_map/mul | solution.py:21
  13.4 35.3 %all-gather.7.cloned.1.call-done = bf16[2048,1024]{1,0:T(8,128)(2,1)} async-done(((bf16[256,1024]{1,0:T(8,128)(2,1)}), bf16[2048,1024]{1,0:T(8,128)(2,1)}) %all-gather.7.cloned.1.call-update) | async-done | bytes 4194320 | tf_op jit(solution)/shard_map/all_gather | solution.py:22
  48.7 9.3 %convolution_convert_fusion.1 = bf16[1024,1024]{1,0:T(8,128)(2,1)} fusion(bf16[1024,2048]{1,0:T(8,128)(2,1)} %bitcast.18, bf16[2048,1024]{1,0:T(8,128)(2,1)} %all-gather.7.cloned.1.call-done), kind=kOutput, calls=%fused_computation.15 | convolution fusion | flops 4296015872 | bytes 10485760 | tf_op jit(solution)/shard_map/dot_general | solution.py:26
  58.0 0.0 all-gather.9.cloned.1.call-update
  58.0 0.0 copy-start.1
  58.0 0.0 reduce-scatter.2.cloned.1.call-start
  58.1 90.0 %all-gather.9.cloned.1.call-done = bf16[4,2048,1024]{2,1,0:T(8,128)(2,1)} async-done(((bf16[4,256,1024]{2,1,0:T(8,128)(2,1)}), bf16[4,2048,1024]{2,1,0:T(8,128)(2,1)}) %all-gather.9.cloned.1.call-update) | async-done | bytes 16777232 | tf_op jit(solution)/shard_map/all_gather | solution.py:30
  148.0 12.3 %convolution_bitcast_fusion = f32[256,2048]{1,0:T(8,128)} fusion(bf16[4,256,1024]{2,1,0:T(8,128)(2,1)} %bitcast.21, bf16[4,2048,1024]{2,1,0:T(8,128)(2,1)} %all-gather.9.cloned.1.call-done), kind=kOutput, calls=%fused_computation.1 | convolution fusion | flops 4294967296 | bytes 20971520 | tf_op jit(solution)/shard_map/pmi,pni->mn/dot_general | solution.py:14
  160.3 0.0 reduce-scatter.2.cloned.1.call-update
  160.3 0.0 all-gather.11.cloned.1.call-start
  160.4 0.5 all-gather.11.cloned.1.call-update
  160.9 0.0 all-gather.17.cloned.1.call-start
  161.0 0.5 all-gather.17.cloned.1.call-update
  161.5 0.0 all-gather.13.cloned.1.call-start
  161.6 42.8 %reduce-scatter.2.cloned.1.call-done = f32[256,512]{1,0:T(8,128)} async-done(((f32[256,2048]{1,0:T(8,128)}), f32[256,512]{1,0:T(8,128)}) %reduce-scatter.2.cloned.1.call-update) | async-done | bytes 524304 | tf_op jit(solution)/shard_map/reduce_scatter | solution.py:34
  204.4 1.8 convert_element_type.49
  206.1 0.0 all-gather.13.cloned.1.call-update
  206.2 0.2 all-gather.15.cloned.1.call-start
  206.4 0.0 copy-done.1
  206.4 0.5 all-gather.15.cloned.1.call-update
  206.9 26.3 %all-gather.11.cloned.1.call-done = bf16[256,2048]{1,0:T(8,128)(2,1)} async-done(((bf16[256,512]{1,0:T(8,128)(2,1)}), bf16[256,2048]{1,0:T(8,128)(2,1)}) %all-gather.11.cloned.1.call-update) | async-done | bytes 1048592 | tf_op jit(solution)/shard_map/all_gather | solution.py:23
  233.2 9.2 %fusion.7 = bf16[256,2048]{1,0:T(8,128)(2,1)} fusion(bf16[2048,1024]{1,0:T(8,128)(2,1)} %all-gather.7.cloned.1.call-done, bf16[1024]{0:T(1024)(128)(2,1)S(1)} %convert_element_type.46, bf16[256,2048]{1,0:T(8,128)(2,1)} %all-gather.11.cloned.1.call-done), kind=kOutput, calls=%fused_computation.9 | convolution fusion | flops 2152464384 | bytes 6293504 | tf_op jit(solution)/shard_map/dot_general | solution.py:10
  242.4 0.0 copy-start
  242.4 20.1 %all-gather.17.cloned.1.call-done = bf16[2048,512]{1,0:T(8,128)(2,1)} async-done(((bf16[256,512]{1,0:T(8,128)(2,1)}), bf16[2048,512]{1,0:T(8,128)(2,1)}) %all-gather.17.cloned.1.call-update) | async-done | bytes 2097168 | tf_op jit(solution)/shard_map/all_gather | solution.py:24
  262.5 8.6 %convolution_convert_fusion = bf16[512,2048]{1,0:T(8,128)(2,1)S(1)} fusion(bf16[2048,1024]{1,0:T(8,128)(2,1)} %all-gather.7.cloned.1.call-done, bf16[1024]{0:T(1024)(128)(2,1)S(1)} %convert_element_type.46, bf16[2048,512]{1,0:T(8,128)(2,1)} %all-gather.17.cloned.1.call-done), kind=kOutput, calls=%fused_computation | convolution fusion | flops 4300734464 | bytes 8390656 | tf_op jit(solution)/shard_map/dot_general | solution.py:10
  271.1 21.2 %all-gather.13.cloned.1.call-done = bf16[2048,512]{1,0:T(8,128)(2,1)} async-done(((bf16[256,512]{1,0:T(8,128)(2,1)}), bf16[2048,512]{1,0:T(8,128)(2,1)}) %all-gather.13.cloned.1.call-update) | async-done | bytes 2097168 | tf_op jit(solution)/shard_map/all_gather | solution.py:36
  292.3 0.0 copy-done
  292.3 2.6 convolution_subtract_fusion.1
  294.9 27.0 %all-gather.15.cloned.1.call-done = bf16[256,2048]{1,0:T(8,128)(2,1)} async-done(((bf16[256,512]{1,0:T(8,128)(2,1)}), bf16[256,2048]{1,0:T(8,128)(2,1)}) %all-gather.15.cloned.1.call-update) | async-done | bytes 1048592 | tf_op jit(solution)/shard_map/all_gather | solution.py:37
  321.9 2.8 convolution_subtract_fusion
  (2 shorter events, 0.0 us)
Async XLA Ops:
  6.5 42.2 %all-gather.7.cloned.1.call-start = ((), (), s32[]{:S(2)}) async-start(), calls=%async_computation.1 | async-start | bytes 4718592 | tf_op jit(solution)/shard_map/all_gather | solution.py:22
  7.3 140.8 %all-gather.9.cloned.1.call-start = ((), (), s32[]{:S(2)}) async-start(), calls=%async_computation.2 | async-start | bytes 18874368 | tf_op jit(solution)/shard_map/all_gather | solution.py:30
  58.0 148.4 %copy-start.1 = (s32[1024]{0:T(1024)S(1)}, s32[1024]{0:T(1024)}, u32[]{:S(2)}) copy-start(s32[1024]{0:T(1024)} %param.9) | copy-start | bytes 12292
  58.0 146.3 %reduce-scatter.2.cloned.1.call-start = ((), (), s32[]{:S(2)}) async-start(), calls=%async_computation.3 | async-start | bytes 2621440 | tf_op jit(solution)/shard_map/reduce_scatter | solution.py:34
  160.3 72.8 %all-gather.11.cloned.1.call-start = ((), (), s32[]{:S(2)}) async-start(), calls=%async_computation.4 | async-start | bytes 1310720 | tf_op jit(solution)/shard_map/all_gather | solution.py:23
  160.9 101.6 %all-gather.17.cloned.1.call-start = ((), (), s32[]{:S(2)}) async-start(), calls=%async_computation.7 | async-start | bytes 2359296 | tf_op jit(solution)/shard_map/all_gather | solution.py:24
  161.5 130.8 %all-gather.13.cloned.1.call-start = ((), (), s32[]{:S(2)}) async-start(), calls=%async_computation.5 | async-start | bytes 2359296 | tf_op jit(solution)/shard_map/all_gather | solution.py:36
  206.2 115.8 %all-gather.15.cloned.1.call-start = ((), (), s32[]{:S(2)}) async-start(), calls=%async_computation.6 | async-start | bytes 1310720 | tf_op jit(solution)/shard_map/all_gather | solution.py:37
  242.4 49.9 %copy-start = (f32[256,512]{1,0:T(8,128)S(1)}, f32[256,512]{1,0:T(8,128)}, u32[]{:S(2)}) copy-start(f32[256,512]{1,0:T(8,128)} %reduce-scatter.2.cloned.1.call-done) | copy-start | bytes 1572868
Sparse Core Ops, SparseCore 0:
  9.2 39.4 all-gather.6
  58.1 89.8 all-gather.8
  160.5 43.8 reduce-scatter.1
  205.9 27.2 all-gather.10
  235.1 27.3 all-gather.16
  264.4 27.8 all-gather.12
  294.0 27.9 all-gather.14

commit v2 on v1

v2 whole, which is shorter than its diff:
```python
import functools

import jax
import jax.numpy as jnp
from jax import lax
from jax.experimental import pallas as pl
from jax.experimental.pallas import tpu as pltpu
from jax.sharding import PartitionSpec as P

ATILE = 32
MESH = pl.DeviceIdType.MESH
BF16 = jnp.bfloat16
F32 = jnp.float32
OF_C, OF_H, OF_K, OF_S = range(4)


def dot_nn(left, right):
    return lax.dot_general(left, right, (((1,), (0,)), ((), ())), preferred_element_type=F32)


def dot_nt(left, right):
    return lax.dot_general(left, right, (((1,), (1,)), ((), ())), preferred_element_type=F32)


def dot_tn(left, right):
    return lax.dot_general(left, right, (((0,), (0,)), ((), ())), preferred_element_type=F32)


def flipped(index, step):
    bit = 1
    while bit <= step:
        if step & bit:
            index = index + bit - 2 * bit * lax.rem(lax.div(index, bit), 2)
        bit *= 2
    return index


def kernel(
    n_grp, n_blk,
    keep_ref, env_ref, orb_ref, margin_ref, slab_hbm, out_ref,
    slab, c_all, acc, h_own, h_buf, zt_send, zt_recv, k_recv,
    k_cols, k_rows, s_cols, s_rows, mid,
    load_sem, dir_s, dir_r, fwd_s, fwd_r, zt_s, zt_r, sum_s, sum_r, kz_s, kz_r, sz_s, sz_r,
):
    z = lax.axis_index("grp")
    b = lax.axis_index("blk")
    n_chip = n_blk // 2
    chip, core = lax.div(b, 2), lax.rem(b, 2)
    sib = chip * 2 + 1 - core
    aux, rows, nao = slab.shape
    half_aux = aux // 2
    width = 2 * rows
    steps = range(1, n_chip)
    sent = []

    load = pltpu.make_async_copy(slab_hbm, slab, load_sem)
    load.start()

    barrier = pltpu.get_barrier_semaphore()
    for s in range(1, n_blk):
        pl.semaphore_signal(barrier, inc=1, device_id=(z, lax.rem(b + s, n_blk)), device_id_type=MESH)
    for s in range(1, n_grp):
        pl.semaphore_signal(barrier, inc=1, device_id=(lax.rem(z + s, n_grp), b), device_id_type=MESH)
    pl.semaphore_wait(barrier, n_blk + n_grp - 2)

    def remote(src, dst, send_sem, recv_sem, to):
        return pltpu.make_async_remote_copy(
            src_ref=src, dst_ref=dst, send_sem=send_sem, recv_sem=recv_sem,
            device_id=to, device_id_type=MESH,
        )

    def send(src, dst, send_sem, recv_sem, to):
        copy = remote(src, dst, send_sem, recv_sem, to)
        copy.start()
        sent.append(copy)

    def arrived(dst, send_sem, recv_sem):
        remote(dst, dst, send_sem, recv_sem, (z, sib)).wait_recv()

    def to_chip(kind, s, src, dst):
        send(src, dst, dir_s.at[kind, s], dir_r.at[kind, s], (z, flipped(chip, s) * 2 + core))

    def from_chip(kind, s, dst):
        arrived(dst, dir_s.at[kind, s], dir_r.at[kind, s])

    def to_sib(kind, s, ref):
        send(ref, ref, fwd_s.at[kind, s], fwd_r.at[kind, s], (z, sib))

    def from_sib(kind, s, dst):
        arrived(dst, fwd_s.at[kind, s], fwd_r.at[kind, s])

    per_acc = acc.shape[2] // rows

    def k_block(j):
        start = pl.multiple_of(lax.rem(j, per_acc) * rows, rows)
        return acc.at[lax.div(j, per_acc), :, pl.ds(start, rows)]

    def t_row(j):
        return slab.at[2, :, pl.ds(pl.multiple_of(j * rows, rows), rows)]

    def t_col(j):
        start = pl.multiple_of(lax.rem(j, n_grp) * width, width)
        return slab.at[lax.div(j, n_grp), :, pl.ds(start, width)]

    def k_send(c):
        return slab.at[3, :, pl.ds(pl.multiple_of(c * width, width), width)]

    def c_block(index):
        return c_all.at[pl.ds(pl.multiple_of(index * rows, rows), rows)]

    c_block(b)[...] = orb_ref[...]
    to_sib(OF_C, 0, c_block(b))
    for s in steps:
        to_chip(OF_C, s, c_block(b), c_block(b))
    s_rows[z] = margin_ref[...]
    s_cols[b] = margin_ref[...]
    for s in range(1, n_grp):
        send(s_rows.at[z], s_rows.at[z], sz_s.at[s], sz_r.at[s], (flipped(z, s), b))

    load.wait()
    tiles = rows // ATILE
    for t in range(tiles):
        keep = jnp.broadcast_to(keep_ref[t : t + 1, :], (ATILE, nao)).astype(BF16)

        @pl.loop(0, aux)
        def _(p):
            slab[p, t * ATILE : (t + 1) * ATILE, :] = slab[p, t * ATILE : (t + 1) * ATILE, :] * keep

    def half_part(p, c):
        start = pl.multiple_of(c * width, width)
        return dot_nn(slab[p, :, pl.ds(start, width)], c_all[pl.ds(start, width), :])

    from_sib(OF_C, 0, c_block(sib))

    for s in steps:
        c_new, c_old = flipped(chip, s), flipped(chip, s - 1)
        from_chip(OF_C, s, c_block(c_new * 2 + core))
        to_sib(OF_C, s, c_block(c_new * 2 + core))

        @pl.loop(0, aux)
        def _(p):
            part = half_part(p, c_old)
            acc[p] = part if s == 1 else acc[p] + part

        from_sib(OF_C, s, c_block(c_new * 2 + 1 - core))

    c_last = flipped(chip, n_chip - 1)

    @pl.loop(0, aux)
    def _(p):
        h_own[p] = (acc[p] + half_part(p, c_last)).astype(BF16)

    def h_slot(c, a):
        return h_buf.at[pl.ds(c * aux + a * half_aux, half_aux)]

    def upper(s):
        top = 1 << (s.bit_length() - 1)
        return lax.rem(lax.div(chip, top), 2)

    for s in steps:
        first = half_aux * (1 - upper(s))
        to_chip(OF_H, s, h_own.at[pl.ds(first, half_aux)], h_slot(chip, core))
    own_slot = h_buf.at[pl.ds(chip * aux, aux)]
    send(h_own, own_slot, fwd_s.at[OF_H, 0], fwd_r.at[OF_H, 0], (z, sib))

    def pair(own_first, other, other_first, count):
        def add(p, total):
            return total + dot_nt(h_own[own_first + p], other[other_first + p])

        return lax.fori_loop(0, count, add, jnp.zeros((rows, rows), F32))

    k_block(b)[...] = pair(0, h_own, 0, aux)

    for s in range(1, n_grp):
        arrived(s_rows.at[flipped(z, s)], sz_s.at[s], sz_r.at[s])
    mid[:rows] = jnp.zeros((rows, mid.shape[1]), F32)

    @pl.loop(0, n_grp)
    def _(g):
        start = pl.multiple_of(g * width, width)
        mid[:rows] += dot_nn(s_rows[g], c_all[pl.ds(start, width), :])

    m_rows = (mid[:rows] * env_ref[...]).astype(BF16)

    @pl.loop(0, n_blk)
    def _(j):
        t_row(j)[...] = dot_nt(m_rows, c_block(j)[...]).astype(BF16)

    from_sib(OF_H, 0, own_slot)
    k_block(sib)[...] = pair(0, h_buf, chip * aux, aux)

    def sum_copy(c):
        return remote(k_send(c), k_recv.at[z], sum_s.at[c], sum_r.at[z], (c, b))

    def finish_chunk(c):
        for a in range(2):
            at = pl.multiple_of(c * width + a * rows, rows)
            slab[3, :, pl.ds(at, rows)] = k_block(2 * c + a)[...].astype(BF16)

        @pl.when(c != z)
        def _():
            sum_copy(c).start()

    finish_chunk(chip)

    def exchange_block(s, a):
        c = flipped(chip, s)
        other = 2 * c + a
        block = pair(half_aux * upper(s), h_buf, c * aux + a * half_aux, half_aux)
        k_block(other)[...] = block
        zt_send[other] = block.T.astype(BF16)
        send(zt_send.at[other], zt_recv.at[b], zt_s.at[2 * s + a], zt_r.at[2 * s + core], (z, other))

    def add_block(s):
        c = flipped(chip, s)
        for a in range(2):
            other = 2 * c + a
            arrived(zt_recv.at[other], zt_s.at[2 * s + a], zt_r.at[2 * s + a])
            k_block(other)[...] += zt_recv[other].astype(F32)
        finish_chunk(c)

    for s in steps:
        c = flipped(chip, s)
        from_chip(OF_H, s, h_slot(c, core))
        to_sib(OF_H, s, h_slot(c, core))
        exchange_block(s, core)
        from_sib(OF_H, s, h_slot(c, 1 - core))
        exchange_block(s, 1 - core)
        if s > 1:
            add_block(s - 1)
    to_sib(OF_S, 0, s_cols.at[b])
    for s in steps:
        to_chip(OF_S, s, s_cols.at[b], s_cols.at[b])
    add_block(n_chip - 1)

    from_sib(OF_S, 0, s_cols.at[sib])
    for s in steps:
        c = flipped(chip, s)
        from_chip(OF_S, s, s_cols.at[2 * c + core])
        to_sib(OF_S, s, s_cols.at[2 * c + core])
    for s in steps:
        from_sib(OF_S, s, s_cols.at[2 * flipped(chip, s) + 1 - core])
    mid[...] = jnp.zeros(mid.shape, F32)

    @pl.loop(0, n_blk)
    def _(j):
        mid[...] += dot_tn(s_cols[j], c_block(j)[...])

    m_cols = (mid[...] * env_ref[...]).astype(BF16)

    @pl.loop(0, n_blk)
    def _(j):
        t_col(j)[...] = dot_nt(c_block(j)[...], m_cols).astype(BF16)

    k_tile = jnp.concatenate([k_block(2 * z)[...], k_block(2 * z + 1)[...]], axis=1)
    for s in range(1, n_grp):
        other = flipped(z, s)
        arrived(k_recv.at[other], sum_s.at[other], sum_r.at[other])
        k_tile = k_tile + k_recv[other].astype(F32)
    k_bf = k_tile.astype(BF16)
    out_ref[...] = k_tile
    k_cols[b] = k_bf
    k_rows[z] = k_bf
    for s in range(1, n_grp):
        send(k_rows.at[z], k_rows.at[z], kz_s.at[s], kz_r.at[s], (flipped(z, s), b))
    to_sib(OF_K, 0, k_cols.at[b])
    for s in steps:
        to_chip(OF_K, s, k_cols.at[b], k_cols.at[b])

    def take_first(j):
        out_ref[...] -= dot_nn(t_row(j)[...], k_cols[j])

    def take_second(g):
        out_ref[...] -= dot_nn(k_rows[g, :, :rows], t_col(2 * g)[...])
        out_ref[...] -= dot_nn(k_rows[g, :, rows:], t_col(2 * g + 1)[...])

    take_first(b)
    take_second(z)
    from_sib(OF_K, 0, k_cols.at[sib])
    take_first(sib)
    for s in steps:
        c = flipped(chip, s)
        from_chip(OF_K, s, k_cols.at[2 * c + core])
        to_sib(OF_K, s, k_cols.at[2 * c + core])
        take_first(2 * c + core)
    for s in steps:
        other = 2 * flipped(chip, s) + 1 - core
        from_sib(OF_K, s, k_cols.at[other])
        take_first(other)
    for s in range(1, n_grp):
        other = flipped(z, s)
        arrived(k_rows.at[other], kz_s.at[s], kz_r.at[s])
        take_second(other)

    for copy in sent:
        copy.wait_send()
    for s in range(n_chip):
        c = flipped(chip, s)

        @pl.when(c != z)
        def _():
            sum_copy(c).wait_send()


def on_device(n_grp, n_blk, slab, block_mask, orbitals, margin, env_flag):
    aux, rows, nao = slab.shape
    occ = orbitals.shape[1]
    width = margin.shape[1]
    n_chip = n_blk // 2
    assert width == 2 * rows and n_chip == n_grp and aux == 4
    keep = jnp.repeat(block_mask[0], ATILE, axis=1).astype(F32)
    env = env_flag.astype(F32)[None, :]
    vmem = pl.BlockSpec(memory_space=pltpu.VMEM)
    dma = pltpu.SemaphoreType.DMA
    return pl.pallas_call(
        functools.partial(kernel, n_grp, n_blk),
        out_shape=jax.ShapeDtypeStruct((rows, width), F32),
        in_specs=[vmem] * 4 + [pl.BlockSpec(memory_space=pl.ANY)],
        out_specs=vmem,
        scratch_shapes=[
            pltpu.VMEM((aux, rows, nao), BF16),
            pltpu.VMEM((nao, occ), BF16),
            pltpu.VMEM((aux, rows, occ), F32),
            pltpu.VMEM((aux, rows, occ), BF16),
            pltpu.VMEM((n_chip * aux, rows, occ), BF16),
            pltpu.VMEM((n_blk, rows, rows), BF16),
            pltpu.VMEM((n_blk, rows, rows), BF16),
            pltpu.VMEM((n_grp, rows, width), BF16),
            pltpu.VMEM((n_blk, rows, width), BF16),
            pltpu.VMEM((n_grp, rows, width), BF16),
            pltpu.VMEM((n_blk, rows, width), BF16),
            pltpu.VMEM((n_grp, rows, width), BF16),
            pltpu.VMEM((width, occ), F32),
            dma(()),
            dma((4, n_chip)), dma((4, n_chip)), dma((4, n_chip)), dma((4, n_chip)),
            dma((2 * n_chip,)), dma((2 * n_chip,)),
            dma((n_grp,)), dma((n_grp,)), dma((n_grp,)), dma((n_grp,)), dma((n_grp,)), dma((n_grp,)),
        ],
        compiler_params=pltpu.CompilerParams(
            collective_id=0, has_side_effects=True, vmem_limit_bytes=63 * 2**20
        ),
    )(keep, env, orbitals, margin, slab)


def solution(mesh):
    placed = (P("grp", "blk", None), P("grp", "blk", None), P("blk", None), P("blk", "grp"), P())
    return jax.shard_map(
        functools.partial(on_device, mesh.shape["grp"], mesh.shape["blk"]),
        mesh=mesh, in_specs=placed, out_specs=P("blk", "grp"), check_vma=False,
    )
```

time: 332 us -> 146 us (0.44)
  waiting for transfers between devices: 265 us -> 0 us
  Pallas kernels: 0 us -> 139 us
  matrix products: 44.8 us -> 0 us
  between operations: 13.6 us -> 0.02 us
  other arithmetic: 7.03 us -> 1.97 us
    all_gather x6 -> x0, waiting for transfers between devices: 220 us -> none  [the longest x1 90 us: on_device(): rows_k = pair_block(half, lax.all_gather(half, 'blk', axis=1, tiled=True))]
    pallas_call x0 -> x1, Pallas kernels: none -> 139 us  [on_device(): pl.pallas_call(functools.partial(kernel, n_grp, n_blk), out_shape=jax.Sha...]
    dot_general x6 -> x0, matrix products: 44.8 us -> none  [the longest x4 23.2 us: dot32(): lax.dot_general(left, right, (dims, ((), ())), preferred_element_type=jnp...]
    reduce_scatter x1 -> x0, waiting for transfers between devices: 42.8 us -> none  [on_device(): k_tile = lax.psum_scatter(rows_k, 'grp', scatter_dimension=1, tiled=True)]
    mul x1 -> x0, other arithmetic: 4.56 us -> none  [on_device(): masked = slab * keep_tile[None, :, :]]
  transfers between devices with their start and end apart: 7 -> 0, of which waited for: 7 -> 0; matrix products, arithmetic and copies ran while one was open for 9% -> 0% of each run, Pallas kernels for 0% -> 0%
where the time goes in v2:
time: 146 us; the launch traced here: 144 us
  Pallas kernels  139 us (95%)
  local copies, waits for them, and re-layouts  2.76 us (2%)
  other arithmetic  1.97 us (1%)
    pallas_call x1, Pallas kernels, on_device(): pl.pallas_call(functools.partial(kernel, n_grp, n_blk), out_shape=jax.Sha...  139 us

profile of v2, /device:TPU:0, one launch (start us, length us, event | category | flops | bytes accessed | tf_op | source)
XLA Modules:
  0.0 143.7 jit_solution(12548383877573171729)
XLA Ops:
  0.0 0.7 convert_bitcast_fusion
  0.7 1.3 convert_element_type.13
  2.0 0.1 broadcast_in_dim.6
  2.1 0.8 convert_element_type.12.keep_ref
  2.9 139.0 %shard_map.55 = f32[256,512]{1,0:T(8,128)} custom-call(f32[8,2048]{1,0:T(8,128)} %convert_element_type.12.keep_ref, f32[1,1024]{1,0:T(1,128)} %bitcast.3, bf16[256,1024]{1,0:T(8,128)(2,1)} %orb_ref.1, bf16[256,512]{1,0:T(8,128)(2,1)} %margin_ref.1, bf16[4,256,2048]{2,1,0:T(8,128)(2,1)} %slab_hbm.1), custom_call_target="tpu_custom_call" | custom-call | tf_op jit(solution)/shard_map/pallas_call | solution.py:315
  141.9 1.9 %copy.7 = f32[256,512]{1,0:T(8,128)} copy(f32[256,512]{1,0:T(8,128)} %shard_map.55) | data formatting | bytes 1048576

commit v3 on v2

--- a/solution.py
+++ b/solution.py
@@ -37,10 +37,10 @@
 
 def kernel(
     n_grp, n_blk,
-    keep_ref, env_ref, orb_ref, margin_ref, slab_hbm, out_ref,
+    mask_ref, env_ref, orb_ref, margin_ref, slab_hbm, out_ref,
     slab, c_all, acc, h_own, h_buf, zt_send, zt_recv, k_recv,
     k_cols, k_rows, s_cols, s_rows, mid,
-    load_sem, dir_s, dir_r, fwd_s, fwd_r, zt_s, zt_r, sum_s, sum_r, kz_s, kz_r, sz_s, sz_r,
+    load_sem, dir_s, dir_r, fwd_s, fwd_r, zt_s, zt_r, sum_s, sum_r, kz_up, kz_down, kz_r, sz_s, sz_r,
 ):
     z = lax.axis_index("grp")
     b = lax.axis_index("blk")
@@ -51,6 +51,9 @@
     half_aux = aux // 2
     width = 2 * rows
     steps = range(1, n_chip)
+    two_hop = n_chip == 4
+    bit1 = lax.div(chip, 2)
+    parity = lax.rem(lax.rem(chip, 2) + bit1, 2)
     sent = []
 
     load = pltpu.make_async_copy(slab_hbm, slab, load_sem)
@@ -77,17 +80,18 @@
     def arrived(dst, send_sem, recv_sem):
         remote(dst, dst, send_sem, recv_sem, (z, sib)).wait_recv()
 
-    def to_chip(kind, s, src, dst):
-        send(src, dst, dir_s.at[kind, s], dir_r.at[kind, s], (z, flipped(chip, s) * 2 + core))
-
-    def from_chip(kind, s, dst):
-        arrived(dst, dir_s.at[kind, s], dir_r.at[kind, s])
-
-    def to_sib(kind, s, ref):
-        send(ref, ref, fwd_s.at[kind, s], fwd_r.at[kind, s], (z, sib))
-
-    def from_sib(kind, s, dst):
-        arrived(dst, fwd_s.at[kind, s], fwd_r.at[kind, s])
+    def to_chip(kind, s, src, dst, i=0, via=None):
+        to = (z, flipped(chip, via or s) * 2 + core)
+        send(src, dst, dir_s.at[kind, s, i], dir_r.at[kind, s, i], to)
+
+    def from_chip(kind, s, dst, i=0):
+        arrived(dst, dir_s.at[kind, s, i], dir_r.at[kind, s, i])
+
+    def to_sib(kind, s, ref, i=0):
+        send(ref, ref, fwd_s.at[kind, s, i], fwd_r.at[kind, s, i], (z, sib))
+
+    def from_sib(kind, s, dst, i=0):
+        arrived(dst, fwd_s.at[kind, s, i], fwd_r.at[kind, s, i])
 
     per_acc = acc.shape[2] // rows
 
@@ -110,17 +114,30 @@
 
     c_block(b)[...] = orb_ref[...]
     to_sib(OF_C, 0, c_block(b))
-    for s in steps:
-        to_chip(OF_C, s, c_block(b), c_block(b))
+
+    def c_half(index, i):
+        start = pl.multiple_of(index * rows + i * (rows // 2), rows // 2)
+        return c_all.at[pl.ds(start, rows // 2)]
+
+    if two_hop:
+        for s, i in ((1, 0), (2, 1), (1, 1), (2, 0)):
+            to_chip(OF_C, s, c_half(b, i), c_half(b, i), i)
+    else:
+        for s in steps:
+            for i in range(2):
+                to_chip(OF_C, s, c_half(b, i), c_half(b, i), i)
     s_rows[z] = margin_ref[...]
     s_cols[b] = margin_ref[...]
     for s in range(1, n_grp):
         send(s_rows.at[z], s_rows.at[z], sz_s.at[s], sz_r.at[s], (flipped(z, s), b))
 
+    spread = lax.broadcasted_iota(jnp.int32, (nao // ATILE, nao), 1)
+    tile = lax.broadcasted_iota(jnp.int32, (nao // ATILE, nao), 0) * ATILE
+    spread = jnp.where((spread >= tile) & (spread < tile + ATILE), 1.0, 0.0).astype(BF16)
+    keep_all = dot_nn(mask_ref[0].astype(F32).astype(BF16), spread)
     load.wait()
-    tiles = rows // ATILE
-    for t in range(tiles):
-        keep = jnp.broadcast_to(keep_ref[t : t + 1, :], (ATILE, nao)).astype(BF16)
+    for t in range(rows // ATILE):
+        keep = jnp.broadcast_to(keep_all[t : t + 1, :], (ATILE, nao)).astype(BF16)
 
         @pl.loop(0, aux)
         def _(p):
@@ -132,36 +149,73 @@
 
     from_sib(OF_C, 0, c_block(sib))
 
-    for s in steps:
-        c_new, c_old = flipped(chip, s), flipped(chip, s - 1)
-        from_chip(OF_C, s, c_block(c_new * 2 + core))
-        to_sib(OF_C, s, c_block(c_new * 2 + core))
-
+    def start_half(c, first):
         @pl.loop(0, aux)
         def _(p):
-            part = half_part(p, c_old)
-            acc[p] = part if s == 1 else acc[p] + part
-
-        from_sib(OF_C, s, c_block(c_new * 2 + 1 - core))
-
+            part = half_part(p, c)
+            acc[p] = part if first else acc[p] + part
+
+    def c_arrives(s, i):
+        from_chip(OF_C, s, c_half(flipped(chip, s) * 2 + core, i), i)
+
+    def c_crosses(s):
+        to_sib(OF_C, s, c_block(flipped(chip, s) * 2 + core))
+
+    if two_hop:
+        for s, i in ((1, 0), (2, 1)):
+            c_arrives(s, i)
+            part = c_half(flipped(chip, s) * 2 + core, i)
+            to_chip(OF_C, 3, part, part, i, via=3 - s)
+    start_half(chip, True)
+    if two_hop:
+        c_arrives(1, 1)
+        c_crosses(1)
+        c_arrives(2, 0)
+        c_crosses(2)
+    else:
+        for s in steps[:-1]:
+            c_arrives(s, 0)
+            c_arrives(s, 1)
+            c_crosses(s)
+    for s in steps[:-1]:
+        from_sib(OF_C, s, c_block(flipped(chip, s) * 2 + 1 - core))
+        start_half(flipped(chip, s), False)
     c_last = flipped(chip, n_chip - 1)
-
-    @pl.loop(0, aux)
-    def _(p):
+    c_arrives(n_chip - 1, 0)
+    c_arrives(n_chip - 1, 1)
+    c_crosses(n_chip - 1)
+    from_sib(OF_C, n_chip - 1, c_block(c_last * 2 + 1 - core))
+
+    def end_half(p):
         h_own[p] = (acc[p] + half_part(p, c_last)).astype(BF16)
 
-    def h_slot(c, a):
-        return h_buf.at[pl.ds(c * aux + a * half_aux, half_aux)]
+    def h_slot(c, a, i):
+        return h_buf.at[c * aux + a * half_aux + i]
 
     def upper(s):
         top = 1 << (s.bit_length() - 1)
         return lax.rem(lax.div(chip, top), 2)
 
-    for s in steps:
-        first = half_aux * (1 - upper(s))
-        to_chip(OF_H, s, h_own.at[pl.ds(first, half_aux)], h_slot(chip, core))
+    def aux_from(s, i):
+        if not two_hop:
+            return half_aux * upper(s) + i
+        ahead = 1 - bit1 if s > 1 else bit1
+        if s == 3:
+            return 2 * (parity if i == 0 else 1 - parity) + ahead
+        return 2 * (1 - parity if s == 1 else parity) + (ahead if i == 0 else 1 - ahead)
+
+    if two_hop:
+        for s, i in ((1, 0), (2, 0), (1, 1), (2, 1)):
+            p = 2 * (parity if s == 1 else 1 - parity) + (bit1 if i == 0 else 1 - bit1)
+            end_half(p)
+            to_chip(OF_H, s, h_own.at[p], h_slot(chip, core, i), i)
+    else:
+        pl.loop(0, aux)(end_half)
+        for s in steps:
+            for i in range(half_aux):
+                to_chip(OF_H, s, h_own.at[half_aux * (1 - upper(s)) + i], h_slot(chip, core, i), i)
     own_slot = h_buf.at[pl.ds(chip * aux, aux)]
-    send(h_own, own_slot, fwd_s.at[OF_H, 0], fwd_r.at[OF_H, 0], (z, sib))
+    send(h_own, own_slot, fwd_s.at[OF_H, 0, 0], fwd_r.at[OF_H, 0, 0], (z, sib))
 
     def pair(own_first, other, other_first, count):
         def add(p, total):
@@ -180,7 +234,7 @@
         start = pl.multiple_of(g * width, width)
         mid[:rows] += dot_nn(s_rows[g], c_all[pl.ds(start, width), :])
 
-    m_rows = (mid[:rows] * env_ref[...]).astype(BF16)
+    m_rows = (mid[:rows] * env_ref[...].astype(F32)).astype(BF16)
 
     @pl.loop(0, n_blk)
     def _(j):
@@ -206,7 +260,7 @@
     def exchange_block(s, a):
         c = flipped(chip, s)
         other = 2 * c + a
-        block = pair(half_aux * upper(s), h_buf, c * aux + a * half_aux, half_aux)
+        block = sum(dot_nt(h_own[aux_from(s, i)], h_slot(c, a, i)[...]) for i in range(half_aux))
         k_block(other)[...] = block
         zt_send[other] = block.T.astype(BF16)
         send(zt_send.at[other], zt_recv.at[b], zt_s.at[2 * s + a], zt_r.at[2 * s + core], (z, other))
@@ -219,15 +273,36 @@
             k_block(other)[...] += zt_recv[other].astype(F32)
         finish_chunk(c)
 
-    for s in steps:
-        c = flipped(chip, s)
-        from_chip(OF_H, s, h_slot(c, core))
-        to_sib(OF_H, s, h_slot(c, core))
+    def h_arrives(s, i):
+        slot = h_slot(flipped(chip, s), core, i)
+        from_chip(OF_H, s, slot, i)
+        if two_hop and s < 3 and i == 0:
+            to_chip(OF_H, 3, slot, h_slot(flipped(chip, s), core, s - 1), s - 1, via=3 - s)
+        to_sib(OF_H, s, slot, i)
+
+    def exchange_step(s):
         exchange_block(s, core)
-        from_sib(OF_H, s, h_slot(c, 1 - core))
+        for i in range(half_aux):
+            from_sib(OF_H, s, h_slot(flipped(chip, s), 1 - core, i), i)
         exchange_block(s, 1 - core)
-        if s > 1:
-            add_block(s - 1)
+
+    if two_hop:
+        for s, i in ((1, 0), (2, 0), (1, 1), (2, 1)):
+            h_arrives(s, i)
+        exchange_step(1)
+        exchange_step(2)
+        add_block(1)
+        add_block(2)
+        h_arrives(3, 0)
+        h_arrives(3, 1)
+        exchange_step(3)
+    else:
+        for s in steps:
+            for i in range(half_aux):
+                h_arrives(s, i)
+            exchange_step(s)
+            if s > 1:
+                add_block(s - 1)
     to_sib(OF_S, 0, s_cols.at[b])
     for s in steps:
         to_chip(OF_S, s, s_cols.at[b], s_cols.at[b])
@@ -246,7 +321,7 @@
     def _(j):
         mid[...] += dot_tn(s_cols[j], c_block(j)[...])
 
-    m_cols = (mid[...] * env_ref[...]).astype(BF16)
+    m_cols = (mid[...] * env_ref[...].astype(F32)).astype(BF16)
 
     @pl.loop(0, n_blk)
     def _(j):
@@ -261,8 +336,26 @@
     out_ref[...] = k_tile
     k_cols[b] = k_bf
     k_rows[z] = k_bf
-    for s in range(1, n_grp):
-        send(k_rows.at[z], k_rows.at[z], kz_s.at[s], kz_r.at[s], (flipped(z, s), b))
+    line = n_grp == 4
+
+    def row_copy(g, sems, to):
+        return remote(k_rows.at[g], k_rows.at[g], sems.at[g], kz_r.at[g], (to, b))
+
+    def pass_rows(g, ahead, wait):
+        def act(copy):
+            copy.wait_send() if wait else copy.start()
+
+        if ahead > 0:
+            pl.when(z < n_grp - 1)(lambda: act(row_copy(g, kz_up, z + 1)))
+        else:
+            pl.when(z > 0)(lambda: act(row_copy(g, kz_down, z - 1)))
+
+    if line:
+        pass_rows(z, 1, False)
+        pass_rows(z, -1, False)
+    else:
+        for s in range(1, n_grp):
+            send(k_rows.at[z], k_rows.at[z], kz_up.at[s], kz_r.at[s], (flipped(z, s), b))
     to_sib(OF_K, 0, k_cols.at[b])
     for s in steps:
         to_chip(OF_K, s, k_cols.at[b], k_cols.at[b])
@@ -273,24 +366,51 @@
     def take_second(g):
         out_ref[...] -= dot_nn(k_rows[g, :, :rows], t_col(2 * g)[...])
         out_ref[...] -= dot_nn(k_rows[g, :, rows:], t_col(2 * g + 1)[...])
+
+    def line_rows(d, wait=False):
+        for ahead in (1, -1):
+            g = z - ahead * d
+
+            @pl.when(z >= d if ahead > 0 else z < n_grp - d)
+            def _():
+                if not wait:
+                    arrived(k_rows.at[g], kz_up.at[g], kz_r.at[g])
+                pass_rows(g, ahead, wait)
+                if not wait:
+                    take_second(g)
+
+    def cols_arrive(s):
+        other = 2 * flipped(chip, s) + core
+        from_chip(OF_K, s, k_cols.at[other])
+        to_sib(OF_K, s, k_cols.at[other])
+        take_first(other)
 
     take_first(b)
     take_second(z)
     from_sib(OF_K, 0, k_cols.at[sib])
     take_first(sib)
-    for s in steps:
-        c = flipped(chip, s)
-        from_chip(OF_K, s, k_cols.at[2 * c + core])
-        to_sib(OF_K, s, k_cols.at[2 * c + core])
-        take_first(2 * c + core)
+    if line:
+        line_rows(1)
+    for s in steps:
+        cols_arrive(s)
+        if line and s == 1:
+            line_rows(2)
     for s in steps:
         other = 2 * flipped(chip, s) + 1 - core
         from_sib(OF_K, s, k_cols.at[other])
         take_first(other)
-    for s in range(1, n_grp):
-        other = flipped(z, s)
-        arrived(k_rows.at[other], kz_s.at[s], kz_r.at[s])
-        take_second(other)
+    if line:
+        line_rows(3)
+        pass_rows(z, 1, True)
+        pass_rows(z, -1, True)
+        line_rows(1, True)
+        line_rows(2, True)
+        line_rows(3, True)
+    else:
+        for s in range(1, n_grp):
+            other = flipped(z, s)
+            arrived(k_rows.at[other], kz_up.at[s], kz_r.at[s])
+            take_second(other)
 
     for copy in sent:
         copy.wait_send()
@@ -308,8 +428,7 @@
     width = margin.shape[1]
     n_chip = n_blk // 2
     assert width == 2 * rows and n_chip == n_grp and aux == 4
-    keep = jnp.repeat(block_mask[0], ATILE, axis=1).astype(F32)
-    env = env_flag.astype(F32)[None, :]
+    env = env_flag[None, :]
     vmem = pl.BlockSpec(memory_space=pltpu.VMEM)
     dma = pltpu.SemaphoreType.DMA
     return pl.pallas_call(
@@ -332,14 +451,15 @@
             pltpu.VMEM((n_grp, rows, width), BF16),
             pltpu.VMEM((width, occ), F32),
             dma(()),
-            dma((4, n_chip)), dma((4, n_chip)), dma((4, n_chip)), dma((4, n_chip)),
+            dma((4, n_chip, 2)), dma((4, n_chip, 2)), dma((4, n_chip, 2)), dma((4, n_chip, 2)),
             dma((2 * n_chip,)), dma((2 * n_chip,)),
             dma((n_grp,)), dma((n_grp,)), dma((n_grp,)), dma((n_grp,)), dma((n_grp,)), dma((n_grp,)),
+            dma((n_grp,)),
         ],
         compiler_params=pltpu.CompilerParams(
             collective_id=0, has_side_effects=True, vmem_limit_bytes=63 * 2**20
         ),
-    )(keep, env, orbitals, margin, slab)
+    )(block_mask, env, orbitals, margin, slab)
 
 
 def solution(mesh):

time: 146 us -> 126 us (0.86); the launches traced: 144 us -> 126 us
  Pallas kernels: 139 us -> 124 us
  other arithmetic: 1.97 us -> 0 us
    pallas_call x1, Pallas kernels: 139 us -> 124 us  [on_device(): pl.pallas_call(functools.partial(kernel, n_grp, n_blk), out_shape=jax.Sha...]
    convert_element_type x2 -> x0, other arithmetic: 1.97 us -> none  [the longest x1 1.28 us: on_device(): env = env_flag.astype(F32)[None, :]]
where the time goes in v3:
time: 126 us
  Pallas kernels  124 us (98%)
  local copies, waits for them, and re-layouts  1.87 us (1%)
    pallas_call x1, Pallas kernels, on_device(): pl.pallas_call(functools.partial(kernel, n_grp, n_blk), out_shape=jax.Sha...  124 us

profile of v3, /device:TPU:0, one launch (start us, length us, event | category | flops | bytes accessed | tf_op | source)
XLA Modules:
  0.0 125.8 jit_solution(3178064029936698749)
XLA Ops:
  0.0 123.9 %shard_map.55 = f32[256,512]{1,0:T(8,128)} custom-call(s32[1,8,64]{2,1,0:T(8,128)} %mask_ref.1, s32[1,1024]{1,0:T(1,128)} %bitcast.1, bf16[256,1024]{1,0:T(8,128)(2,1)} %orb_ref.1, bf16[256,512]{1,0:T(8,128)(2,1)} %margin_ref.1, bf16[4,256,2048]{2,1,0:T(8,128)(2,1)} %slab_hbm.1), custom_call_target="tpu_custom_call" | custom-call | tf_op jit(solution)/shard_map/pallas_call | solution.py:434
  123.9 1.9 %copy.7 = f32[256,512]{1,0:T(8,128)} copy(f32[256,512]{1,0:T(8,128)} %shard_map.55) | data formatting | bytes 1048576

commit v4 on v3

--- a/solution.py
+++ b/solution.py
@@ -276,8 +276,6 @@
     def h_arrives(s, i):
         slot = h_slot(flipped(chip, s), core, i)
         from_chip(OF_H, s, slot, i)
-        if two_hop and s < 3 and i == 0:
-            to_chip(OF_H, 3, slot, h_slot(flipped(chip, s), core, s - 1), s - 1, via=3 - s)
         to_sib(OF_H, s, slot, i)
 
     def exchange_step(s):
@@ -289,6 +287,9 @@
     if two_hop:
         for s, i in ((1, 0), (2, 0), (1, 1), (2, 1)):
             h_arrives(s, i)
+        for s in (1, 2):
+            c = flipped(chip, s)
+            to_chip(OF_H, 3, h_slot(c, core, 0), h_slot(c, core, s - 1), s - 1, via=3 - s)
         exchange_step(1)
         exchange_step(2)
         add_block(1)
@@ -303,29 +304,27 @@
             exchange_step(s)
             if s > 1:
                 add_block(s - 1)
+    add_block(n_chip - 1)
     to_sib(OF_S, 0, s_cols.at[b])
     for s in steps:
         to_chip(OF_S, s, s_cols.at[b], s_cols.at[b])
-    add_block(n_chip - 1)
-
+
+    def add_margin(j):
+        mid[...] += dot_tn(s_cols[j], c_block(j)[...])
+
+    mid[...] = dot_tn(s_cols[b], c_block(b)[...])
     from_sib(OF_S, 0, s_cols.at[sib])
-    for s in steps:
-        c = flipped(chip, s)
-        from_chip(OF_S, s, s_cols.at[2 * c + core])
-        to_sib(OF_S, s, s_cols.at[2 * c + core])
-    for s in steps:
-        from_sib(OF_S, s, s_cols.at[2 * flipped(chip, s) + 1 - core])
-    mid[...] = jnp.zeros(mid.shape, F32)
-
-    @pl.loop(0, n_blk)
-    def _(j):
-        mid[...] += dot_tn(s_cols[j], c_block(j)[...])
-
+    add_margin(sib)
+    for s in steps:
+        other = 2 * flipped(chip, s)
+        from_chip(OF_S, s, s_cols.at[other + core])
+        to_sib(OF_S, s, s_cols.at[other + core])
+        add_margin(other + core)
+    for s in steps:
+        other = 2 * flipped(chip, s) + 1 - core
+        from_sib(OF_S, s, s_cols.at[other])
+        add_margin(other)
     m_cols = (mid[...] * env_ref[...].astype(F32)).astype(BF16)
-
-    @pl.loop(0, n_blk)
-    def _(j):
-        t_col(j)[...] = dot_nt(c_block(j)[...], m_cols).astype(BF16)
 
     k_tile = jnp.concatenate([k_block(2 * z)[...], k_block(2 * z + 1)[...]], axis=1)
     for s in range(1, n_grp):
@@ -359,6 +358,10 @@
     to_sib(OF_K, 0, k_cols.at[b])
     for s in steps:
         to_chip(OF_K, s, k_cols.at[b], k_cols.at[b])
+
+    @pl.loop(0, n_blk)
+    def _(j):
+        t_col(j)[...] = dot_nt(c_block(j)[...], m_cols).astype(BF16)
 
     def take_first(j):
         out_ref[...] -= dot_nn(t_row(j)[...], k_cols[j])

time: 126 us -> 123 us (0.976)
  Pallas kernels: 124 us -> 120 us
    pallas_call x1, Pallas kernels: 124 us -> 120 us  [on_device(): pl.pallas_call(functools.partial(kernel, n_grp, n_blk), out_shape=jax.Sha...]
where the time goes in v4:
time: 123 us; the launch traced here: 122 us
  Pallas kernels  120 us (98%)
  local copies, waits for them, and re-layouts  1.87 us (2%)
    pallas_call x1, Pallas kernels, on_device(): pl.pallas_call(functools.partial(kernel, n_grp, n_blk), out_shape=jax.Sha...  120 us

profile of v4, /device:TPU:0, one launch (start us, length us, event | category | flops | bytes accessed | tf_op | source)
XLA Modules:
  0.0 122.4 jit_solution(3707825988439422260)
XLA Ops:
  0.0 120.5 %shard_map.55 = f32[256,512]{1,0:T(8,128)} custom-call(s32[1,8,64]{2,1,0:T(8,128)} %mask_ref.1, s32[1,1024]{1,0:T(1,128)} %bitcast.1, bf16[256,1024]{1,0:T(8,128)(2,1)} %orb_ref.1, bf16[256,512]{1,0:T(8,128)(2,1)} %margin_ref.1, bf16[4,256,2048]{2,1,0:T(8,128)(2,1)} %slab_hbm.1), custom_call_target="tpu_custom_call" | custom-call | tf_op jit(solution)/shard_map/pallas_call | solution.py:437
  120.5 1.9 %copy.7 = f32[256,512]{1,0:T(8,128)} copy(f32[256,512]{1,0:T(8,128)} %shard_map.55) | data formatting | bytes 1048576

commit v5 on v4

--- a/solution.py
+++ b/solution.py
@@ -37,7 +37,7 @@
 
 def kernel(
     n_grp, n_blk,
-    mask_ref, env_ref, orb_ref, margin_ref, slab_hbm, out_ref,
+    mask_ref, env_ref, orb_ref, margin_ref, slab_hbm, tile_ref, fix_ref,
     slab, c_all, acc, h_own, h_buf, zt_send, zt_recv, k_recv,
     k_cols, k_rows, s_cols, s_rows, mid,
     load_sem, dir_s, dir_r, fwd_s, fwd_r, zt_s, zt_r, sum_s, sum_r, kz_up, kz_down, kz_r, sz_s, sz_r,
@@ -181,13 +181,24 @@
         from_sib(OF_C, s, c_block(flipped(chip, s) * 2 + 1 - core))
         start_half(flipped(chip, s), False)
     c_last = flipped(chip, n_chip - 1)
-    c_arrives(n_chip - 1, 0)
-    c_arrives(n_chip - 1, 1)
-    c_crosses(n_chip - 1)
-    from_sib(OF_C, n_chip - 1, c_block(c_last * 2 + 1 - core))
+    near, far = c_last * 2 + core, c_last * 2 + 1 - core
+    for i in range(2):
+        c_arrives(n_chip - 1, i)
+        to_sib(OF_C, n_chip - 1, c_half(near, i), i)
+
+    def block_part(p, j):
+        start = pl.multiple_of(j * rows, rows)
+        return dot_nn(slab[p, :, pl.ds(start, rows)], c_block(j)[...])
+
+    @pl.loop(0, aux)
+    def _(p):
+        acc[p] = acc[p] + block_part(p, near)
+
+    for i in range(2):
+        from_sib(OF_C, n_chip - 1, c_half(far, i), i)
 
     def end_half(p):
-        h_own[p] = (acc[p] + half_part(p, c_last)).astype(BF16)
+        h_own[p] = (acc[p] + block_part(p, far)).astype(BF16)
 
     def h_slot(c, a, i):
         return h_buf.at[c * aux + a * half_aux + i]
@@ -204,11 +215,15 @@
             return 2 * (parity if i == 0 else 1 - parity) + ahead
         return 2 * (1 - parity if s == 1 else parity) + (ahead if i == 0 else 1 - ahead)
 
+    def aux_to(s, i):
+        return 2 * (parity if s == 1 else 1 - parity) + (bit1 if i == 0 else 1 - bit1)
+
     if two_hop:
-        for s, i in ((1, 0), (2, 0), (1, 1), (2, 1)):
-            p = 2 * (parity if s == 1 else 1 - parity) + (bit1 if i == 0 else 1 - bit1)
-            end_half(p)
-            to_chip(OF_H, s, h_own.at[p], h_slot(chip, core, i), i)
+        for s, i in ((1, 0), (2, 0)):
+            end_half(aux_to(s, i))
+            to_chip(OF_H, s, h_own.at[aux_to(s, i)], h_slot(chip, core, i), i)
+        for s, i in ((1, 1), (2, 1)):
+            end_half(aux_to(s, i))
     else:
         pl.loop(0, aux)(end_half)
         for s in steps:
@@ -285,18 +300,24 @@
         exchange_block(s, 1 - core)
 
     if two_hop:
-        for s, i in ((1, 0), (2, 0), (1, 1), (2, 1)):
-            h_arrives(s, i)
         for s in (1, 2):
             c = flipped(chip, s)
-            to_chip(OF_H, 3, h_slot(c, core, 0), h_slot(c, core, s - 1), s - 1, via=3 - s)
+            slot = h_slot(c, core, 0)
+            from_chip(OF_H, s, slot)
+            to_chip(OF_H, 3, slot, h_slot(c, core, s - 1), s - 1, via=3 - s)
+        for s in (1, 2):
+            to_chip(OF_H, s, h_own.at[aux_to(s, 1)], h_slot(chip, core, 1), 1)
+            to_sib(OF_H, s, h_slot(flipped(chip, s), core, 0))
+        h_arrives(3, 0)
+        h_arrives(3, 1)
+        exchange_step(3)
+        add_block(3)
+        h_arrives(1, 1)
+        h_arrives(2, 1)
         exchange_step(1)
         exchange_step(2)
         add_block(1)
         add_block(2)
-        h_arrives(3, 0)
-        h_arrives(3, 1)
-        exchange_step(3)
     else:
         for s in steps:
             for i in range(half_aux):
@@ -304,7 +325,7 @@
             exchange_step(s)
             if s > 1:
                 add_block(s - 1)
-    add_block(n_chip - 1)
+        add_block(n_chip - 1)
     to_sib(OF_S, 0, s_cols.at[b])
     for s in steps:
         to_chip(OF_S, s, s_cols.at[b], s_cols.at[b])
@@ -332,7 +353,7 @@
         arrived(k_recv.at[other], sum_s.at[other], sum_r.at[other])
         k_tile = k_tile + k_recv[other].astype(F32)
     k_bf = k_tile.astype(BF16)
-    out_ref[...] = k_tile
+    tile_ref[...] = k_tile
     k_cols[b] = k_bf
     k_rows[z] = k_bf
     line = n_grp == 4
@@ -364,11 +385,11 @@
         t_col(j)[...] = dot_nt(c_block(j)[...], m_cols).astype(BF16)
 
     def take_first(j):
-        out_ref[...] -= dot_nn(t_row(j)[...], k_cols[j])
+        fix_ref[...] += dot_nn(t_row(j)[...], k_cols[j])
 
     def take_second(g):
-        out_ref[...] -= dot_nn(k_rows[g, :, :rows], t_col(2 * g)[...])
-        out_ref[...] -= dot_nn(k_rows[g, :, rows:], t_col(2 * g + 1)[...])
+        fix_ref[...] += dot_nn(k_rows[g, :, :rows], t_col(2 * g)[...])
+        fix_ref[...] += dot_nn(k_rows[g, :, rows:], t_col(2 * g + 1)[...])
 
     def line_rows(d, wait=False):
         for ahead in (1, -1):
@@ -388,7 +409,7 @@
         to_sib(OF_K, s, k_cols.at[other])
         take_first(other)
 
-    take_first(b)
+    fix_ref[...] = dot_nn(t_row(b)[...], k_bf)
     take_second(z)
     from_sib(OF_K, 0, k_cols.at[sib])
     take_first(sib)
@@ -434,11 +455,11 @@
     env = env_flag[None, :]
     vmem = pl.BlockSpec(memory_space=pltpu.VMEM)
     dma = pltpu.SemaphoreType.DMA
-    return pl.pallas_call(
+    tile, fix = pl.pallas_call(
         functools.partial(kernel, n_grp, n_blk),
-        out_shape=jax.ShapeDtypeStruct((rows, width), F32),
+        out_shape=[jax.ShapeDtypeStruct((rows, width), F32)] * 2,
         in_specs=[vmem] * 4 + [pl.BlockSpec(memory_space=pl.ANY)],
-        out_specs=vmem,
+        out_specs=[vmem, vmem],
         scratch_shapes=[
             pltpu.VMEM((aux, rows, nao), BF16),
             pltpu.VMEM((nao, occ), BF16),
@@ -463,6 +484,7 @@
             collective_id=0, has_side_effects=True, vmem_limit_bytes=63 * 2**20
         ),
     )(block_mask, env, orbitals, margin, slab)
+    return tile - fix
 
 
 def solution(mesh):

time: 123 us -> 125 us (1.016)
  Pallas kernels: 120 us -> 123 us
  other arithmetic: 0 us -> 2.07 us
  local copies, waits for them, and re-layouts: 1.87 us -> 0 us
    pallas_call x1, Pallas kernels: 120 us -> 123 us  [on_device(): pl.pallas_call(functools.partial(kernel, n_grp, n_blk), out_shape=[jax.Sh...]
    sub x0 -> x1, other arithmetic: none -> 2.07 us  [on_device(): return tile - fix]
    unnamed x1 -> x0, local copies, waits for them, and re-layouts: 1.87 us -> none
where the time goes in v5:
time: 125 us
  Pallas kernels  123 us (98%)
  other arithmetic  2.07 us (2%)
    pallas_call x1, Pallas kernels, on_device(): pl.pallas_call(functools.partial(kernel, n_grp, n_blk), out_shape=[jax.Sh...  123 us

profile of v5, /device:TPU:0, one launch (start us, length us, event | category | flops | bytes accessed | tf_op | source)
XLA Modules:
  0.0 124.6 jit_solution(10616167359812928684)
XLA Ops:
  0.0 122.6 %shard_map.55 = (f32[256,512]{1,0:T(8,128)}, f32[256,512]{1,0:T(8,128)}) custom-call(s32[1,8,64]{2,1,0:T(8,128)} %mask_ref.1, s32[1,1024]{1,0:T(1,128)} %bitcast.1, bf16[256,1024]{1,0:T(8,128)(2,1)} %orb_ref.1, bf16[256,512]{1,0:T(8,128)(2,1)} %margin_ref.1, bf16[4,256,2048]{2,1,0:T(8,128)(2,1)} %slab_hbm.1), custom_call_target="tpu_custom_call" | custom-call | tf_op jit(solution)/shard_map/pallas_call | solution.py:458
  122.6 2.1 %sub.3 = f32[256,512]{1,0:T(8,128)} subtract(f32[256,512]{1,0:T(8,128)} %get-tuple-element.7, f32[256,512]{1,0:T(8,128)} %get-tuple-element.8) | non-fusion elementwise | flops 131072 | bytes 1572864 | tf_op jit(solution)/shard_map/sub | solution.py:487

commit v6 on v4

--- a/solution.py
+++ b/solution.py
@@ -39,8 +39,8 @@
     n_grp, n_blk,
     mask_ref, env_ref, orb_ref, margin_ref, slab_hbm, out_ref,
     slab, c_all, acc, h_own, h_buf, zt_send, zt_recv, k_recv,
-    k_cols, k_rows, s_cols, s_rows, mid,
-    load_sem, dir_s, dir_r, fwd_s, fwd_r, zt_s, zt_r, sum_s, sum_r, kz_up, kz_down, kz_r, sz_s, sz_r,
+    k_cols, k_rows, s_cols, s_rows, mid, k_far,
+    load_sem, dir_s, dir_r, fwd_s, fwd_r, zt_s, zt_r, sum_s, sum_r, kz_up, kz_down, kz_r, sz_s, sz_r, far_s, far_r,
 ):
     z = lax.axis_index("grp")
     b = lax.axis_index("blk")
@@ -181,13 +181,24 @@
         from_sib(OF_C, s, c_block(flipped(chip, s) * 2 + 1 - core))
         start_half(flipped(chip, s), False)
     c_last = flipped(chip, n_chip - 1)
-    c_arrives(n_chip - 1, 0)
-    c_arrives(n_chip - 1, 1)
-    c_crosses(n_chip - 1)
-    from_sib(OF_C, n_chip - 1, c_block(c_last * 2 + 1 - core))
+    near, far = c_last * 2 + core, c_last * 2 + 1 - core
+    for i in range(2):
+        c_arrives(n_chip - 1, i)
+        to_sib(OF_C, n_chip - 1, c_half(near, i), i)
+
+    def block_part(p, j):
+        start = pl.multiple_of(j * rows, rows)
+        return dot_nn(slab[p, :, pl.ds(start, rows)], c_block(j)[...])
+
+    @pl.loop(0, aux)
+    def _(p):
+        acc[p] = acc[p] + block_part(p, near)
+
+    for i in range(2):
+        from_sib(OF_C, n_chip - 1, c_half(far, i), i)
 
     def end_half(p):
-        h_own[p] = (acc[p] + half_part(p, c_last)).astype(BF16)
+        h_own[p] = (acc[p] + block_part(p, far)).astype(BF16)
 
     def h_slot(c, a, i):
         return h_buf.at[c * aux + a * half_aux + i]
@@ -204,11 +215,13 @@
             return 2 * (parity if i == 0 else 1 - parity) + ahead
         return 2 * (1 - parity if s == 1 else parity) + (ahead if i == 0 else 1 - ahead)
 
+    def aux_to(s, i):
+        return 2 * (parity if s == 1 else 1 - parity) + (bit1 if i == 0 else 1 - bit1)
+
     if two_hop:
         for s, i in ((1, 0), (2, 0), (1, 1), (2, 1)):
-            p = 2 * (parity if s == 1 else 1 - parity) + (bit1 if i == 0 else 1 - bit1)
-            end_half(p)
-            to_chip(OF_H, s, h_own.at[p], h_slot(chip, core, i), i)
+            end_half(aux_to(s, i))
+            to_chip(OF_H, s, h_own.at[aux_to(s, i)], h_slot(chip, core, i), i)
     else:
         pl.loop(0, aux)(end_half)
         for s in steps:
@@ -246,14 +259,35 @@
     def sum_copy(c):
         return remote(k_send(c), k_recv.at[z], sum_s.at[c], sum_r.at[z], (c, b))
 
+    line = n_grp == 4 and n_chip == 4
+    adder = (z == 1) | (z == 2)
+    far_end = n_grp - 1 - z if not line else jnp.where(z == 1, 3, 0)
+
+    def is_far(c):
+        return (c - z == 3) | (z - c == 3)
+
+    def far_copy(c):
+        return remote(k_send(c), k_far, far_s, far_r, (jnp.where(z == 0, 1, 2), b))
+
+    def chunk_part(c, a):
+        return slab.at[3, :, pl.ds(pl.multiple_of(c * width + a * rows, rows), rows)]
+
     def finish_chunk(c):
+        @pl.when(jnp.logical_not(adder & (c == far_end)) if line else c >= 0)
+        def _():
+            for a in range(2):
+                chunk_part(c, a)[...] = k_block(2 * c + a)[...].astype(BF16)
+            if line:
+                pl.when(is_far(c))(lambda: far_copy(c).start())
+            near = (c != z) & jnp.logical_not(is_far(c)) if line else c != z
+            pl.when(near)(lambda: sum_copy(c).start())
+
+    def add_far():
+        arrived(k_far, far_s, far_r)
         for a in range(2):
-            at = pl.multiple_of(c * width + a * rows, rows)
-            slab[3, :, pl.ds(at, rows)] = k_block(2 * c + a)[...].astype(BF16)
-
-        @pl.when(c != z)
-        def _():
-            sum_copy(c).start()
+            part = k_block(2 * far_end + a)[...] + k_far[:, a * rows : (a + 1) * rows].astype(F32)
+            chunk_part(far_end, a)[...] = part.astype(BF16)
+        sum_copy(far_end).start()
 
     finish_chunk(chip)
 
@@ -304,7 +338,11 @@
             exchange_step(s)
             if s > 1:
                 add_block(s - 1)
+    if line:
+        pl.when(adder & (far_end != flipped(chip, n_chip - 1)))(add_far)
     add_block(n_chip - 1)
+    if line:
+        pl.when(adder & (far_end == flipped(chip, n_chip - 1)))(add_far)
     to_sib(OF_S, 0, s_cols.at[b])
     for s in steps:
         to_chip(OF_S, s, s_cols.at[b], s_cols.at[b])
@@ -326,17 +364,21 @@
         add_margin(other)
     m_cols = (mid[...] * env_ref[...].astype(F32)).astype(BF16)
 
-    k_tile = jnp.concatenate([k_block(2 * z)[...], k_block(2 * z + 1)[...]], axis=1)
+    out_ref[:, :rows] = k_block(2 * z)[...]
+    out_ref[:, rows:] = k_block(2 * z + 1)[...]
+
+    def add_sum(other):
+        arrived(k_recv.at[other], sum_s.at[other], sum_r.at[other])
+        out_ref[...] += k_recv[other].astype(F32)
+
     for s in range(1, n_grp):
-        other = flipped(z, s)
-        arrived(k_recv.at[other], sum_s.at[other], sum_r.at[other])
-        k_tile = k_tile + k_recv[other].astype(F32)
-    k_bf = k_tile.astype(BF16)
-    out_ref[...] = k_tile
+        if line and s == 3:
+            pl.when(adder)(lambda: add_sum(flipped(z, 3)))
+        else:
+            add_sum(flipped(z, s))
+    k_bf = out_ref[...].astype(BF16)
     k_cols[b] = k_bf
     k_rows[z] = k_bf
-    line = n_grp == 4
-
     def row_copy(g, sems, to):
         return remote(k_rows.at[g], k_rows.at[g], sems.at[g], kz_r.at[g], (to, b))
 
@@ -420,9 +462,10 @@
     for s in range(n_chip):
         c = flipped(chip, s)
 
-        @pl.when(c != z)
-        def _():
-            sum_copy(c).wait_send()
+        if line:
+            pl.when(is_far(c))(lambda: far_copy(c).wait_send())
+        near = (c != z) & jnp.logical_not(is_far(c)) if line else c != z
+        pl.when(near)(lambda: sum_copy(c).wait_send())
 
 
 def on_device(n_grp, n_blk, slab, block_mask, orbitals, margin, env_flag):
@@ -453,11 +496,12 @@
             pltpu.VMEM((n_blk, rows, width), BF16),
             pltpu.VMEM((n_grp, rows, width), BF16),
             pltpu.VMEM((width, occ), F32),
+            pltpu.VMEM((rows, width), BF16),
             dma(()),
             dma((4, n_chip, 2)), dma((4, n_chip, 2)), dma((4, n_chip, 2)), dma((4, n_chip, 2)),
             dma((2 * n_chip,)), dma((2 * n_chip,)),
             dma((n_grp,)), dma((n_grp,)), dma((n_grp,)), dma((n_grp,)), dma((n_grp,)), dma((n_grp,)),
-            dma((n_grp,)),
+            dma((n_grp,)), dma(()), dma(()),
         ],
         compiler_params=pltpu.CompilerParams(
             collective_id=0, has_side_effects=True, vmem_limit_bytes=63 * 2**20

time: 123 us -> 131 us (1.065)
  Pallas kernels: 120 us -> 128 us
    pallas_call x1, Pallas kernels: 120 us -> 128 us  [on_device(): pl.pallas_call(functools.partial(kernel, n_grp, n_blk), out_shape=jax.Sha...]
where the time goes in v6:
time: 131 us; the launch traced here: 130 us
  Pallas kernels  128 us (98%)
  local copies, waits for them, and re-layouts  1.87 us (1%)
    pallas_call x1, Pallas kernels, on_device(): pl.pallas_call(functools.partial(kernel, n_grp, n_blk), out_shape=jax.Sha...  128 us

profile of v6, /device:TPU:0, one launch (start us, length us, event | category | flops | bytes accessed | tf_op | source)
XLA Modules:
  0.0 130.4 jit_solution(13449465919971483522)
XLA Ops:
  0.0 128.5 %shard_map.55 = f32[256,512]{1,0:T(8,128)} custom-call(s32[1,8,64]{2,1,0:T(8,128)} %mask_ref.1, s32[1,1024]{1,0:T(1,128)} %bitcast.1, bf16[256,1024]{1,0:T(8,128)(2,1)} %orb_ref.1, bf16[256,512]{1,0:T(8,128)(2,1)} %margin_ref.1, bf16[4,256,2048]{2,1,0:T(8,128)(2,1)} %slab_hbm.1), custom_call_target="tpu_custom_call" | custom-call | tf_op jit(solution)/shard_map/pallas_call | solution.py:480
  128.5 1.9 %copy.7 = f32[256,512]{1,0:T(8,128)} copy(f32[256,512]{1,0:T(8,128)} %shard_map.55) | data formatting | bytes 1048576

commit v7 on v4

--- a/solution.py
+++ b/solution.py
@@ -40,7 +40,7 @@
     mask_ref, env_ref, orb_ref, margin_ref, slab_hbm, out_ref,
     slab, c_all, acc, h_own, h_buf, zt_send, zt_recv, k_recv,
     k_cols, k_rows, s_cols, s_rows, mid,
-    load_sem, dir_s, dir_r, fwd_s, fwd_r, zt_s, zt_r, sum_s, sum_r, kz_up, kz_down, kz_r, sz_s, sz_r,
+    load_sem, dir_s, dir_r, fwd_s, fwd_r, zt_s, zt_r, sum_s, sum_r, kz_s, kz_r, sz_s, sz_r,
 ):
     z = lax.axis_index("grp")
     b = lax.axis_index("blk")
@@ -309,6 +309,34 @@
     for s in steps:
         to_chip(OF_S, s, s_cols.at[b], s_cols.at[b])
 
+    def tile_copies():
+        copies = []
+        for s in range(1, n_grp):
+            to = (flipped(z, s), b)
+            copies.append(remote(k_rows.at[z], k_rows.at[z], kz_s.at[s], kz_r.at[s], to))
+        mine = k_cols.at[b]
+        copies.append(remote(mine, mine, fwd_s.at[OF_K, 0, 0], fwd_r.at[OF_K, 0, 0], (z, sib)))
+        for s in steps:
+            to = (z, flipped(chip, s) * 2 + core)
+            copies.append(remote(mine, mine, dir_s.at[OF_K, s, 0], dir_r.at[OF_K, s, 0], to))
+        return copies
+
+    def finish_tile():
+        out_ref[:, :rows] = k_block(2 * z)[...]
+        out_ref[:, rows:] = k_block(2 * z + 1)[...]
+        for s in range(1, n_grp):
+            other = flipped(z, s)
+            arrived(k_recv.at[other], sum_s.at[other], sum_r.at[other])
+            out_ref[...] += k_recv[other].astype(F32)
+        k_bf = out_ref[...].astype(BF16)
+        k_cols[b] = k_bf
+        k_rows[z] = k_bf
+        for copy in tile_copies():
+            copy.start()
+
+    last = flipped(chip, n_chip - 1)
+    pl.when(z != last)(finish_tile)
+
     def add_margin(j):
         mid[...] += dot_tn(s_cols[j], c_block(j)[...])
 
@@ -326,38 +354,7 @@
         add_margin(other)
     m_cols = (mid[...] * env_ref[...].astype(F32)).astype(BF16)
 
-    k_tile = jnp.concatenate([k_block(2 * z)[...], k_block(2 * z + 1)[...]], axis=1)
-    for s in range(1, n_grp):
-        other = flipped(z, s)
-        arrived(k_recv.at[other], sum_s.at[other], sum_r.at[other])
-        k_tile = k_tile + k_recv[other].astype(F32)
-    k_bf = k_tile.astype(BF16)
-    out_ref[...] = k_tile
-    k_cols[b] = k_bf
-    k_rows[z] = k_bf
-    line = n_grp == 4
-
-    def row_copy(g, sems, to):
-        return remote(k_rows.at[g], k_rows.at[g], sems.at[g], kz_r.at[g], (to, b))
-
-    def pass_rows(g, ahead, wait):
-        def act(copy):
-            copy.wait_send() if wait else copy.start()
-
-        if ahead > 0:
-            pl.when(z < n_grp - 1)(lambda: act(row_copy(g, kz_up, z + 1)))
-        else:
-            pl.when(z > 0)(lambda: act(row_copy(g, kz_down, z - 1)))
-
-    if line:
-        pass_rows(z, 1, False)
-        pass_rows(z, -1, False)
-    else:
-        for s in range(1, n_grp):
-            send(k_rows.at[z], k_rows.at[z], kz_up.at[s], kz_r.at[s], (flipped(z, s), b))
-    to_sib(OF_K, 0, k_cols.at[b])
-    for s in steps:
-        to_chip(OF_K, s, k_cols.at[b], k_cols.at[b])
+    pl.when(z == last)(finish_tile)
 
     @pl.loop(0, n_blk)
     def _(j):
@@ -369,18 +366,6 @@
     def take_second(g):
         out_ref[...] -= dot_nn(k_rows[g, :, :rows], t_col(2 * g)[...])
         out_ref[...] -= dot_nn(k_rows[g, :, rows:], t_col(2 * g + 1)[...])
-
-    def line_rows(d, wait=False):
-        for ahead in (1, -1):
-            g = z - ahead * d
-
-            @pl.when(z >= d if ahead > 0 else z < n_grp - d)
-            def _():
-                if not wait:
-                    arrived(k_rows.at[g], kz_up.at[g], kz_r.at[g])
-                pass_rows(g, ahead, wait)
-                if not wait:
-                    take_second(g)
 
     def cols_arrive(s):
         other = 2 * flipped(chip, s) + core
@@ -392,29 +377,19 @@
     take_second(z)
     from_sib(OF_K, 0, k_cols.at[sib])
     take_first(sib)
-    if line:
-        line_rows(1)
     for s in steps:
         cols_arrive(s)
-        if line and s == 1:
-            line_rows(2)
     for s in steps:
         other = 2 * flipped(chip, s) + 1 - core
         from_sib(OF_K, s, k_cols.at[other])
         take_first(other)
-    if line:
-        line_rows(3)
-        pass_rows(z, 1, True)
-        pass_rows(z, -1, True)
-        line_rows(1, True)
-        line_rows(2, True)
-        line_rows(3, True)
-    else:
-        for s in range(1, n_grp):
-            other = flipped(z, s)
-            arrived(k_rows.at[other], kz_up.at[s], kz_r.at[s])
-            take_second(other)
-
+    for s in range(1, n_grp):
+        other = flipped(z, s)
+        arrived(k_rows.at[other], kz_s.at[s], kz_r.at[s])
+        take_second(other)
+
+    for copy in tile_copies():
+        copy.wait_send()
     for copy in sent:
         copy.wait_send()
     for s in range(n_chip):
@@ -457,7 +432,6 @@
             dma((4, n_chip, 2)), dma((4, n_chip, 2)), dma((4, n_chip, 2)), dma((4, n_chip, 2)),
             dma((2 * n_chip,)), dma((2 * n_chip,)),
             dma((n_grp,)), dma((n_grp,)), dma((n_grp,)), dma((n_grp,)), dma((n_grp,)), dma((n_grp,)),
-            dma((n_grp,)),
         ],
         compiler_params=pltpu.CompilerParams(
             collective_id=0, has_side_effects=True, vmem_limit_bytes=63 * 2**20

time: 123 us -> 122 us (level)
  no operation moved by 1% of the time
where the time goes in v7:
time: 122 us
  Pallas kernels  120 us (98%)
  local copies, waits for them, and re-layouts  1.87 us (2%)
    pallas_call x1, Pallas kernels, on_device(): pl.pallas_call(functools.partial(kernel, n_grp, n_blk), out_shape=jax.Sha...  120 us

profile of v7, /device:TPU:0, one launch (start us, length us, event | category | flops | bytes accessed | tf_op | source)
XLA Modules:
  0.0 121.9 jit_solution(1113509523543128709)
XLA Ops:
  0.0 120.0 %shard_map.55 = f32[256,512]{1,0:T(8,128)} custom-call(s32[1,8,64]{2,1,0:T(8,128)} %mask_ref.1, s32[1,1024]{1,0:T(1,128)} %bitcast.1, bf16[256,1024]{1,0:T(8,128)(2,1)} %orb_ref.1, bf16[256,512]{1,0:T(8,128)(2,1)} %margin_ref.1, bf16[4,256,2048]{2,1,0:T(8,128)(2,1)} %slab_hbm.1), custom_call_target="tpu_custom_call" | custom-call | tf_op jit(solution)/shard_map/pallas_call | solution.py:412
  120.1 1.9 %copy.7 = f32[256,512]{1,0:T(8,128)} copy(f32[256,512]{1,0:T(8,128)} %shard_map.55) | data formatting | bytes 1048576
